TPU v7x, 512 devices: a whole 4x8x8 slice. The times are simulated.
512 devices in a mesh: store: 64 (over y, x, core), mp: 8 (over z).
Axes of the slice: x: 4, y: 8, z: 8, core: 2. Of those that a mesh axis runs over, the one named last changes fastest.
Arguments:
- queries: bfloat16 [32768, 8192], P(('store', 'mp')), may hold values from -6 to 6
- question_keys: bfloat16 [32768, 1024], P(('store', 'mp')), may hold values from -6 to 6
- question_values: bfloat16 [32768, 1024], P(('store', 'mp')), may hold values from -6 to 6
- stored_keys: bfloat16 [512, 128, 1024], P('store', None, 'mp'), may hold values from -6 to 6
- stored_values: bfloat16 [512, 128, 1024], P('store', None, 'mp'), may hold values from -6 to 6
- storage_row: int32 [512], replicated, may hold values from 0 to 511, as said below
- retrieved: int32 [256, 16], P('store'), may hold values from 0 to 511, as said below
Outputs:
- attended: bfloat16 [32768, 8192], P(('store', 'mp'))
Inputs may be any that keep to these rules, and one draw needn't show every extreme that they name: storage_row is a permutation; the block at storage row p is held by store index p // 8. `retrieved`: the 4 requests s * 4 to s * 4 + 3 together retrieve 64 blocks held by 64 different store indices, one block from each.
All inputs are finite; a program needn't handle non-finite values.
Results may differ from a plain program's by a relative error of at most 0.009.
Values may be sent and summed in bfloat16 or wider, within the bound.
A program may use at most 64 MiB of HBM per device.

v0:
```python
import math

import jax
import jax.numpy as jnp
from jax import lax
from jax.sharding import PartitionSpec as P

HEAD_SIZE = 128
HEAD_GROUP = 8
REQUEST_TOKENS = 128


def near_part(query_rows, nearby_keys, token_count):
    scale = 1.0 / math.sqrt(HEAD_SIZE)
    near_scores = jnp.dot(query_rows, nearby_keys.T, preferred_element_type=jnp.float32) * scale
    row_token = jnp.arange(token_count * HEAD_GROUP) // HEAD_GROUP
    causal = jnp.arange(token_count)[None, :] <= row_token[:, None]
    return (jnp.where(causal, near_scores, -jnp.inf), causal)


def attend_head(
    query_rows, nearby_keys, nearby_values, remote_keys, remote_values, token_count, order
):
    scale = 1.0 / math.sqrt(HEAD_SIZE)
    near_scores, causal = near_part(query_rows, nearby_keys, token_count)
    start_max = jnp.max(near_scores, axis=1)
    near_weights = jnp.where(causal, jnp.exp(near_scores - start_max[:, None]), 0.0)
    start_total = jnp.sum(near_weights, axis=1)
    start_sum = jnp.dot(
        near_weights.astype(jnp.bfloat16), nearby_values, preferred_element_type=jnp.float32
    )

    def absorb(carry, holder):
        running_max, running_total, running_sum = carry
        block_keys = remote_keys[holder]
        block_values = remote_values[holder]
        scores = jnp.dot(query_rows, block_keys.T, preferred_element_type=jnp.float32) * scale
        new_max = jnp.maximum(running_max, jnp.max(scores, axis=1))
        shrink = jnp.exp(running_max - new_max)
        weights = jnp.exp(scores - new_max[:, None])
        new_total = running_total * shrink + jnp.sum(weights, axis=1)
        new_sum = running_sum * shrink[:, None] + jnp.dot(
            weights.astype(jnp.bfloat16), block_values, preferred_element_type=jnp.float32
        )
        return ((new_max, new_total, new_sum), None)

    final, unused = lax.scan(absorb, (start_max, start_total, start_sum), order)
    return (
        (final[2] / final[1][:, None])
        .astype(jnp.bfloat16)
        .reshape(token_count, HEAD_GROUP * HEAD_SIZE)
    )


def local(
    queries, question_keys, question_values, stored_keys, stored_values, storage_row, retrieved
):
    query_part, key_part, value_part = (
        lax.all_to_all(queries, "mp", split_axis=1, concat_axis=0, tiled=True),
        lax.all_to_all(question_keys, "mp", split_axis=1, concat_axis=0, tiled=True),
        lax.all_to_all(question_values, "mp", split_axis=1, concat_axis=0, tiled=True),
    )
    held = stored_keys.shape[0]
    own_index = lax.axis_index("store")
    store_count = lax.axis_size("store")
    request_count = retrieved.shape[0]
    topc_count = retrieved.shape[1]
    rows_mine = storage_row[retrieved.reshape(-1)]
    owner_mine = rows_mine // held
    all_lists = lax.all_gather(retrieved, "store", axis=0, tiled=True)
    all_rows = storage_row[all_lists.reshape(store_count, request_count * topc_count)]
    matched = all_rows // held == own_index
    wanted = jnp.sum(jnp.where(matched, all_rows % held + 1, 0), axis=1) - 1
    picked = jnp.maximum(wanted, 0)
    send_keys = stored_keys[picked]
    send_values = stored_values[picked]
    owner_table = owner_mine.reshape(request_count, topc_count)
    token_count = REQUEST_TOKENS
    width = HEAD_GROUP * HEAD_SIZE
    blocks = []
    fetched_keys, fetched_values = (
        lax.all_to_all(send_keys, "store", split_axis=0, concat_axis=0, tiled=True),
        lax.all_to_all(send_values, "store", split_axis=0, concat_axis=0, tiled=True),
    )
    for request in range(request_count):
        lower = request * token_count
        upper = lower + token_count
        query_rows = query_part[lower:upper, 0:width].reshape(token_count * HEAD_GROUP, HEAD_SIZE)
        nearby_keys = key_part[lower:upper, 0:HEAD_SIZE]
        nearby_values = value_part[lower:upper, 0:HEAD_SIZE]
        query_rows, nearby_keys, nearby_values = (query_rows, nearby_keys, nearby_values)
        pieces = attend_head(
            query_rows,
            nearby_keys,
            nearby_values,
            fetched_keys,
            fetched_values,
            token_count,
            owner_table[request],
        )
        blocks.append(pieces)
    result = jnp.concatenate(blocks, axis=0)
    return lax.all_to_all(result, "mp", split_axis=0, concat_axis=1, tiled=True)


def solution(mesh):
    return jax.shard_map(
        local,
        mesh=mesh,
        in_specs=(
            P(("store", "mp"), None),
            P(("store", "mp"), None),
            P(("store", "mp"), None),
            P("store", None, "mp"),
            P("store", None, "mp"),
            P(),
            P("store", None),
        ),
        out_specs=P(("store", "mp"), None),
        check_vma=False,
    )
```

profile of v0, /device:TPU:8, one launch (start us, length us, event | category | flops | bytes accessed | tf_op | source)
XLA Modules:
  0.0 592.1 jit_solution(7433230943649113645)
XLA Ops:
  0.0 1.6 copy_bitcast_fusion.2
  1.6 10.3 %all-to-all-start.1 = ((bf16[64,8,128]{2,0,1:T(8,128)(2,1)}), bf16[64,8,128]{2,0,1:T(8,128)(2,1)S(1)}, u32[]{:S(2)}, u32[]{:S(2)}) async-start(bf16[64,8,128]{2,0,1:T(8,128)(2,1)} %copy_bitcast_fusion.2), calls=%async_computation.1 | async-start | bytes 262144 | tf_op jit(solution)/shard_map/all_to_all | solution.py:60
  11.9 1.6 copy_bitcast_fusion.1
  13.5 7.5 %all-to-all-done.1 = bf16[64,8,128]{2,0,1:T(8,128)(2,1)S(1)} async-done(((bf16[64,8,128]{2,0,1:T(8,128)(2,1)}), bf16[64,8,128]{2,0,1:T(8,128)(2,1)S(1)}, u32[]{:S(2)}, u32[]{:S(2)}) %all-to-all-start.1) | async-done | bytes 131104 | tf_op jit(solution)/shard_map/all_to_all | solution.py:60
  21.0 3.4 all-to-all-start.2
  24.4 2.3 copy.42
  26.7 6.7 %all-to-all-done.2 = bf16[64,8,128]{2,0,1:T(8,128)(2,1)S(1)} async-done(((bf16[64,8,128]{2,0,1:T(8,128)(2,1)}), bf16[64,8,128]{2,0,1:T(8,128)(2,1)S(1)}, u32[]{:S(2)}, u32[]{:S(2)}) %all-to-all-start.2) | async-done | bytes 131104 | tf_op jit(solution)/shard_map/all_to_all | solution.py:61
  33.4 3.6 all-to-all-start
  37.0 49.8 %all-gather = s32[64,4,16]{2,1,0:T(4,128)S(1)} all-gather(s32[1,4,16]{2,1,0:T(4,128)S(1)} %bitcast.134), channel_id=1, replica_groups=mesh['store'=64,'mp'=8] {'store'}, dimensions={0}, use_global_device_ids=true | all-gather | bytes 16640 | tf_op jit(solution)/shard_map/all_gather | solution.py:70
  87.1 25.9 %gather_fusion.1 = s32[4096]{0:T(1024)S(1)} fusion(s32[512]{0:T(512)S(1)} %copy-done.1, s32[4096]{0:T(1024)S(1)} %broadcast_clamp_fusion), kind=kCustom, calls=%fused_computation.1 | custom fusion | bytes 49152 | tf_op jit(solution)/shard_map/gather | solution.py:71
  113.2 2.1 gather_fusion.3
  115.3 8.7 %all-to-all-start.4 = ((bf16[64,128,128]{2,1,0:T(8,128)(2,1)}), bf16[64,128,128]{2,1,0:T(8,128)(2,1)}, u32[]{:S(2)}, u32[]{:S(2)}) async-start(bf16[64,128,128]{2,1,0:T(8,128)(2,1)} %gather_fusion.3), calls=%async_computation.4 | async-start | bytes 4194304 | tf_op jit(solution)/shard_map/all_to_all | solution.py:83
  124.0 2.1 gather_fusion.2
  126.1 48.2 %all-to-all-done.4 = bf16[64,128,128]{2,1,0:T(8,128)(2,1)} async-done(((bf16[64,128,128]{2,1,0:T(8,128)(2,1)}), bf16[64,128,128]{2,1,0:T(8,128)(2,1)}, u32[]{:S(2)}, u32[]{:S(2)}) %all-to-all-start.4) | async-done | bytes 2097184 | tf_op jit(solution)/shard_map/all_to_all | solution.py:83
  174.3 6.5 %all-to-all-start.3 = ((bf16[64,128,128]{2,1,0:T(8,128)(2,1)}), bf16[64,128,128]{2,1,0:T(8,128)(2,1)}, u32[]{:S(2)}, u32[]{:S(2)}) async-start(bf16[64,128,128]{2,1,0:T(8,128)(2,1)} %gather_fusion.2), calls=%async_computation.3 | async-start | bytes 4194304 | tf_op jit(solution)/shard_map/all_to_all | solution.py:82
  186.8 44.3 %all-to-all-done.3 = bf16[64,128,128]{2,1,0:T(8,128)(2,1)} async-done(((bf16[64,128,128]{2,1,0:T(8,128)(2,1)}), bf16[64,128,128]{2,1,0:T(8,128)(2,1)}, u32[]{:S(2)}, u32[]{:S(2)}) %all-to-all-start.3) | async-done | bytes 2097184 | tf_op jit(solution)/shard_map/all_to_all | solution.py:82
  231.1 88.0 %while.59 = (s32[]{:T(128)}, f32[1024]{0:T(1024)S(1)}, f32[1024]{0:T(1024)S(1)}, f32[1024,128]{1,0:T(8,128)S(1)}, s32[16]{0:T(128)}, /*index=5*/bf16[64,128,128]...) while((s32[]{:T(128)}, f32[1024]{0:T(1024)S(1)}, ...), condition=%wide.region_24.25_spmd, body=%wide.region_21.24_spmd.sunk | while | flops 68159488 | bytes 3014827 | solution.py:47
  319.4 78.3 %while.58 = (s32[]{:T(128)}, f32[1024]{0:T(1024)S(1)}, f32[1024]{0:T(1024)S(1)}, f32[1024,128]{1,0:T(8,128)S(1)}, s32[16]{0:T(128)S(1)}, /*index=5*/bf16[64,128,...) while((s32[]{:T(128)}, f32[1024]{0:T(1024)S(1)}, ...), condition=%wide.region_18.19_spmd, body=%wide.region_15.18_spmd.sunk | while | flops 68159488 | bytes 3014827 | solution.py:47
  332.9 1.2 convolution_add_fusion.10
  391.6 1.2 convolution_add_fusion.10
  398.0 78.3 %while.57 = (s32[]{:T(128)}, f32[1024]{0:T(1024)S(1)}, f32[1024]{0:T(1024)S(1)}, f32[1024,128]{1,0:T(8,128)S(1)}, s32[16]{0:T(128)S(1)}, /*index=5*/bf16[64,128,...) while((s32[]{:T(128)}, f32[1024]{0:T(1024)S(1)}, ...), condition=%wide.region_12.13_spmd, body=%wide.region_9.12_spmd.sunk | while | flops 68159488 | bytes 3014827 | solution.py:47
  416.4 1.2 convolution_add_fusion.9
  476.7 78.3 %while.56 = (s32[]{:T(128)}, f32[1024]{0:T(1024)S(1)}, f32[1024]{0:T(1024)S(1)}, f32[1024,128]{1,0:T(8,128)S(1)}, s32[16]{0:T(128)S(1)}, /*index=5*/bf16[64,128,...) while((s32[]{:T(128)}, f32[1024]{0:T(1024)S(1)}, ...), condition=%wide.region_6.7_spmd, body=%wide.region_3.6_spmd.sunk | while | flops 68159488 | bytes 3014827 | solution.py:47
  555.4 35.6 %all_to_all.77 = bf16[8,64,1024]{2,1,0:T(8,128)(2,1)S(1)} all-to-all(bf16[8,64,1024]{2,1,0:T(8,128)(2,1)S(1)} %bitcast.121), channel_id=1, replica_groups=mesh['store'=64,'mp'=8] {'mp'}, dimensions={0} | all-to-all | bytes 2097152 | tf_op jit(solution)/shard_map/all_to_all | solution.py:103
  (504 shorter events, 200.0 us)
Async XLA Ops:
  0.0 113.2 %copy-start = (bf16[8,128,128]{2,1,0:T(8,128)(2,1)S(1)}, bf16[8,128,128]{2,1,0:T(8,128)(2,1)}, u32[]{:S(2)}) copy-start(bf16[8,128,128]{2,1,0:T(8,128)(2,1)} %param.19) | copy-start | bytes 786436
  1.6 19.4 %all-to-all-start.1 = ((bf16[64,8,128]{2,0,1:T(8,128)(2,1)}), bf16[64,8,128]{2,0,1:T(8,128)(2,1)S(1)}, u32[]{:S(2)}, u32[]{:S(2)}) async-start(bf16[64,8,128]{2,0,1:T(8,128)(2,1)} %copy_bitcast_fusion.2), calls=%async_computation.1 | async-start | bytes 262144 | tf_op jit(solution)/shard_map/all_to_all | solution.py:60
  21.0 12.4 %all-to-all-start.2 = ((bf16[64,8,128]{2,0,1:T(8,128)(2,1)}), bf16[64,8,128]{2,0,1:T(8,128)(2,1)S(1)}, u32[]{:S(2)}, u32[]{:S(2)}) async-start(bf16[64,8,128]{2,0,1:T(8,128)(2,1)} %copy_bitcast_fusion.1), calls=%async_computation.2 | async-start | bytes 262144 | tf_op jit(solution)/shard_map/all_to_all | solution.py:61
  24.4 12.6 %copy-start.7 = (s32[4,16]{1,0:T(4,128)S(1)}, s32[4,16]{1,0:T(4,128)}, u32[]{:S(2)}) copy-start(s32[4,16]{1,0:T(4,128)} %param.21) | copy-start | bytes 772
  24.4 62.6 %copy-start.1 = (s32[512]{0:T(512)S(1)}, s32[512]{0:T(512)}, u32[]{:S(2)}) copy-start(s32[512]{0:T(512)} %param.20) | copy-start | bytes 6148
  33.4 81.9 %all-to-all-start = ((bf16[64,8,1024]{2,0,1:T(8,128)(2,1)}), bf16[64,8,1024]{2,0,1:T(8,128)(2,1)S(1)}, u32[]{:S(2)}, u32[]{:S(2)}) async-start(bf16[64,8,1024]{2,0,1:T(8,128)(2,1)} %bitcast.87), calls=%async_computation | async-start | bytes 2097152 | tf_op jit(solution)/shard_map/all_to_all | solution.py:59
  115.3 8.7 %copy-start.2 = (bf16[8,128,128]{2,1,0:T(8,128)(2,1)S(1)}, bf16[8,128,128]{2,1,0:T(8,128)(2,1)}, u32[]{:S(2)}) copy-start(bf16[8,128,128]{2,1,0:T(8,128)(2,1)} %param.18) | copy-start | bytes 786436
  115.3 59.0 %all-to-all-start.4 = ((bf16[64,128,128]{2,1,0:T(8,128)(2,1)}), bf16[64,128,128]{2,1,0:T(8,128)(2,1)}, u32[]{:S(2)}, u32[]{:S(2)}) async-start(bf16[64,128,128]{2,1,0:T(8,128)(2,1)} %gather_fusion.3), calls=%async_computation.4 | async-start | bytes 4194304 | tf_op jit(solution)/shard_map/all_to_all | solution.py:83
  174.3 56.8 %all-to-all-start.3 = ((bf16[64,128,128]{2,1,0:T(8,128)(2,1)}), bf16[64,128,128]{2,1,0:T(8,128)(2,1)}, u32[]{:S(2)}, u32[]{:S(2)}) async-start(bf16[64,128,128]{2,1,0:T(8,128)(2,1)} %gather_fusion.2), calls=%async_computation.3 | async-start | bytes 4194304 | tf_op jit(solution)/shard_map/all_to_all | solution.py:82
  183.6 0.8 copy-start.6
  183.6 1.0 copy-start.5
  183.8 1.2 copy-start.4
  184.7 0.9 copy-start.3
where the time goes:
time: 603 us; the launch traced here: 592 us
  matrix products  143 us (24%)
  loops' own time  128 us (21%)
  waiting for transfers between devices  107 us (18%)
  local copies, waits for them, and re-layouts  88.2 us (15%)
  blocking collectives  85.5 us (14%)
  starting transfers between devices  32.4 us (5%)
  other arithmetic  8.39 us (1%)
    another operation x4, loops' own time, attend_head(): final, unused = lax.scan(absorb, (start_max, start_total, start_sum), order)  128 us
    dot_general x64, matrix products, absorb(): jnp.dot(weights.astype(jnp.bfloat16), block_values, preferred_element_typ...  76.6 us
    dot_general x64, matrix products, absorb(): jnp.dot(query_rows, block_keys.T, preferred_element_type=jnp.float32)  64 us
    all_gather x1, blocking collectives, local(): all_lists = lax.all_gather(retrieved, 'store', axis=0, tiled=True)  49.8 us
    all_to_all x1, waiting for transfers between devices, local(): lax.all_to_all(send_values, 'store', split_axis=0, concat_axis=0, tiled=T...  48.2 us
    dynamic_slice x64, local copies, waits for them, and re-layouts, attend_head(): final, unused = lax.scan(absorb, (start_max, start_total, start_sum), order)  47.3 us
    all_to_all x1, waiting for transfers between devices, local(): lax.all_to_all(send_keys, 'store', split_axis=0, concat_axis=0, tiled=True)  44.3 us
    all_to_all x1, blocking collectives, local(): return lax.all_to_all(result, 'mp', split_axis=0, concat_axis=1, tiled=True)  35.6 us
  transfers between devices with their start and end apart: 5, of which 4 were waited for; matrix products, arithmetic and copies ran while one was open for 7% of the time, Pallas kernels for 0%

commit v1 on v0

v1 whole, which is shorter than its diff:
```python
import functools
import math

import jax
import jax.numpy as jnp
from jax import lax
from jax.experimental import pallas as pl
from jax.experimental.pallas import tpu as pltpu
from jax.sharding import PartitionSpec as P

HEAD = 128
GROUP = 8
TOKENS = 128
CORES = 2
X_CHIPS = 4
HEADS_AT_ONCE = 2
EXPONENT = math.log2(math.e) / math.sqrt(HEAD)
MESH = pl.DeviceIdType.MESH
BF16 = jnp.bfloat16
F32 = jnp.float32


def score_dot(a, b):
    return lax.dot_general(a, b, (((1,), (1,)), ((), ())), preferred_element_type=F32)


def kernel(
    sizes,
    storage_row,
    retrieved,
    queries,
    question_keys,
    question_values,
    stored_keys,
    stored_values,
    out,
    *scratch,
):
    n_y, n_x, n_z, requests, picked = sizes
    ring = n_y // 2
    members = n_x * CORES
    halves = n_z // requests
    part = TOKENS // halves
    width = GROUP * HEAD
    (
        table,
        tables,
        tables_smem,
        stage,
        recv,
        q_all,
        kn_all,
        vn_all,
        o_stage,
        scores,
        local_sem,
        table_send,
        table_recv,
        ring_send,
        ring_recv,
        blk_send,
        blk_recv,
        z_send,
        z_recv,
        o_send,
        o_recv,
    ) = scratch[:21]
    up_keys, up_values, down_keys, down_values = (
        scratch[21 + ring * i : 21 + ring * (i + 1)] for i in range(4)
    )

    store = lax.axis_index("store")
    z = lax.axis_index("mp")
    y = store // members
    member = store % members
    y_up = lax.rem(y + 1, n_y) * members + member
    y_down = lax.rem(y + n_y - 1, n_y) * members + member

    def peer(j):
        return y * members + lax.rem(member + j, members)

    def z_peer(j):
        return lax.rem(z + j, n_z)

    barrier = pltpu.get_barrier_semaphore()
    for target in (y_up, y_down):
        pl.semaphore_signal(barrier, inc=1, device_id=(target, z), device_id_type=MESH)
    for j in range(1, members):
        pl.semaphore_signal(barrier, inc=1, device_id=(peer(j), z), device_id_type=MESH)
    for j in range(1, n_z):
        pl.semaphore_signal(barrier, inc=1, device_id=(store, z_peer(j)), device_id_type=MESH)

    lane = lax.broadcasted_iota(jnp.int32, (8, 128), 1)

    def note(i, value):
        row = storage_row[retrieved[i // picked, lax.rem(i, picked)]]
        return jnp.where(lane == row // 8, lax.rem(row, 8), value)

    table[...] = lax.fori_loop(0, requests * picked, note, jnp.zeros((8, 128), jnp.int32))
    pl.semaphore_wait(barrier, 2 + members - 1 + n_z - 1)

    def remote(src, dst, send, recv_sem, device):
        return pltpu.make_async_remote_copy(
            src_ref=src,
            dst_ref=dst,
            send_sem=send,
            recv_sem=recv_sem,
            device_id=device,
            device_id_type=MESH,
        )

    def table_copy(j):
        return remote(
            table, tables.at[member], table_send.at[j], table_recv.at[j], (peer(j), z)
        )

    for j in range(1, members):
        table_copy(j).start()

    def ring_copy(step, way, kind):
        bufs = ((up_keys, up_values), (down_keys, down_values))[way][kind]
        src = (stored_keys, stored_values)[kind] if step == 1 else bufs[step - 2]
        return remote(
            src,
            bufs[step - 1],
            ring_send.at[step - 1, way, kind],
            ring_recv.at[step - 1, way, kind],
            ((y_up, y_down)[way], z),
        )

    def in_ring(step, way, kind):
        return step < ring or (step == ring and way == kind)

    for kind in range(2):
        for way in range(2):
            if in_ring(1, way, kind):
                ring_copy(1, way, kind).start()

    def z_copies(j):
        to = z_peer(j)
        wide = pl.ds(pl.multiple_of(to * width, width), width)
        narrow = pl.ds(pl.multiple_of(to * HEAD, HEAD), HEAD)
        return [
            remote(src, dst, z_send.at[j, n], z_recv.at[j, n], (store, to))
            for n, (src, dst) in enumerate(
                (
                    (queries.at[:, wide], q_all.at[z]),
                    (question_keys.at[:, narrow], kn_all.at[z]),
                    (question_values.at[:, narrow], vn_all.at[z]),
                )
            )
        ]

    for j in range(1, n_z):
        for copy in z_copies(j):
            copy.start()
    wide = pl.ds(pl.multiple_of(z * width, width), width)
    narrow = pl.ds(pl.multiple_of(z * HEAD, HEAD), HEAD)
    own = [
        pltpu.make_async_copy(queries.at[:, wide], q_all.at[z], local_sem.at[0]),
        pltpu.make_async_copy(question_keys.at[:, narrow], kn_all.at[z], local_sem.at[1]),
        pltpu.make_async_copy(question_values.at[:, narrow], vn_all.at[z], local_sem.at[2]),
    ]
    for copy in own:
        copy.start()

    tables[member] = table[...]
    for j in range(1, members):
        table_copy(j).wait()
    to_smem = pltpu.make_async_copy(tables, tables_smem, local_sem.at[3])
    to_smem.start()
    to_smem.wait()

    def block_copy(slot, holder, j):
        return remote(
            stage.at[slot, j],
            recv.at[holder],
            blk_send.at[slot, j],
            blk_recv.at[slot, j],
            (peer(j), z),
        )

    def hand_out(slot, offset, keys, values):
        holder = lax.rem(y + n_y + offset, n_y) * members + member

        def one(j, carry):
            pick = tables_smem[lax.rem(member + j, members), 0, holder]
            stage[slot, j, 0] = keys[pick]
            stage[slot, j, 1] = values[pick]
            block_copy(slot, holder, j).start()
            return carry

        lax.fori_loop(1, members, one, 0)
        pick = tables_smem[member, 0, holder]
        recv[holder, 0] = keys[pick]
        recv[holder, 1] = values[pick]

    hand_out(0, 0, stored_keys, stored_values)
    for step in range(1, ring + 1):
        for kind in range(2):
            for way in range(2):
                if in_ring(step, way, kind):
                    ring_copy(step, way, kind).wait_recv()
                    if step < ring and in_ring(step + 1, way, kind):
                        ring_copy(step + 1, way, kind).start()
        if step < ring:
            hand_out(2 * step - 1, -step, up_keys[step - 1], up_values[step - 1])
            hand_out(2 * step, step, down_keys[step - 1], down_values[step - 1])
        else:
            hand_out(2 * step - 1, step, up_keys[step - 1], down_values[step - 1])

    for j in range(1, n_z):
        for copy in z_copies(j):
            copy.wait()
    for copy in own:
        copy.wait()
    for step in range(1, ring + 1):
        for kind in range(2):
            for way in range(2):
                if in_ring(step, way, kind):
                    ring_copy(step, way, kind).wait_send()

    def drain(i, carry):
        block_copy(i // (members - 1), 0, 1 + lax.rem(i, members - 1)).wait()
        return carry

    lax.fori_loop(0, n_y * (members - 1), drain, 0)

    rows = HEADS_AT_ONCE * TOKENS
    far = picked * HEAD

    def attend(request):
        holders = [storage_row[retrieved[request, k]] // 8 for k in range(picked)]
        mine = pl.ds(request * halves, halves)

        def chunk(c, carry):
            columns = [
                pl.ds(pl.multiple_of((c * HEADS_AT_ONCE + i) * HEAD, HEAD), HEAD)
                for i in range(HEADS_AT_ONCE)
            ]
            q = jnp.concatenate(
                [q_all[mine, :, cols].reshape(TOKENS, HEAD) for cols in columns], axis=0
            )
            near = score_dot(q, kn_all[mine].reshape(TOKENS, HEAD))
            token = lax.rem(lax.broadcasted_iota(jnp.int32, (rows, TOKENS), 0), TOKENS)
            key = lax.broadcasted_iota(jnp.int32, (rows, TOKENS), 1)
            near = jnp.where(key <= token, near, -jnp.inf)
            scores[:, far : far + HEAD] = near
            top = near
            for k in range(0, picked, 2):
                pair = jnp.concatenate([recv[holders[k], 0], recv[holders[k + 1], 0]], axis=0)
                s = score_dot(q, pair)
                scores[:, k * HEAD : (k + 2) * HEAD] = s
                top = jnp.maximum(top, jnp.maximum(s[:, :HEAD], s[:, HEAD:]))
            top = jnp.max(top, axis=1, keepdims=True)
            w = jnp.exp2((scores[:, far : far + HEAD] - top) * EXPONENT)
            total = w
            summed = jnp.dot(
                w.astype(BF16), vn_all[mine].reshape(TOKENS, HEAD), preferred_element_type=F32
            )
            for k in range(0, picked, 2):
                pair = jnp.concatenate([recv[holders[k], 1], recv[holders[k + 1], 1]], axis=0)
                w = jnp.exp2((scores[:, k * HEAD : (k + 2) * HEAD] - top) * EXPONENT)
                total = total + (w[:, :HEAD] + w[:, HEAD:])
                summed = summed + jnp.dot(w.astype(BF16), pair, preferred_element_type=F32)
            result = (summed / jnp.sum(total, axis=1, keepdims=True)).astype(BF16)
            for i, cols in enumerate(columns):
                o_stage[mine, :, cols] = result[i * TOKENS : (i + 1) * TOKENS].reshape(
                    halves, part, HEAD
                )
            return carry

        lax.fori_loop(0, GROUP // HEADS_AT_ONCE, chunk, 0)

    base = z // halves
    here = lax.rem(z, halves)
    wide = pl.ds(pl.multiple_of(z * width, width), width)

    def out_copy(source, target):
        return remote(
            o_stage.at[target],
            out.at[:, wide],
            o_send.at[target],
            o_recv.at[source],
            (store, target),
        )

    for i in range(1, requests + 1):
        request = lax.rem(base + i, requests)
        attend(request)
        if i < requests:
            for half in range(halves):
                out_copy(z, request * halves + half).start()
        else:
            keep = pltpu.make_async_copy(o_stage.at[z], out.at[:, wide], local_sem.at[4])
            keep.start()
            for j in range(1, halves):
                out_copy(z, base * halves + lax.rem(here + j, halves)).start()
    keep.wait()
    for j in range(1, n_z):
        out_copy(z, z_peer(j)).wait_send()
        out_copy(z_peer(j), z_peer(j)).wait_recv()


def local(queries, question_keys, question_values, stored_keys, stored_values, storage_row, retrieved):
    n_store, n_z = lax.axis_size("store"), lax.axis_size("mp")
    n_x = X_CHIPS
    members = n_x * CORES
    n_y = n_store // members
    requests, picked = retrieved.shape
    ring = n_y // 2
    part = queries.shape[0]
    width = GROUP * HEAD
    held = stored_keys.shape
    dma = pltpu.SemaphoreType.DMA
    scratch = [
        pltpu.VMEM((8, 128), jnp.int32),
        pltpu.VMEM((members, 8, 128), jnp.int32),
        pltpu.SMEM((members, 8, 128), jnp.int32),
        pltpu.VMEM((n_y, members, 2, TOKENS, HEAD), BF16),
        pltpu.VMEM((n_store, 2, TOKENS, HEAD), BF16),
        pltpu.VMEM((n_z, part, width), BF16),
        pltpu.VMEM((n_z, part, HEAD), BF16),
        pltpu.VMEM((n_z, part, HEAD), BF16),
        pltpu.VMEM((n_z, part, width), BF16),
        pltpu.VMEM((HEADS_AT_ONCE * TOKENS, (picked + 1) * HEAD), F32),
        dma((5,)),
        dma((members,)),
        dma((members,)),
        dma((ring, 2, 2)),
        dma((ring, 2, 2)),
        dma((n_y, members)),
        dma((n_y, members)),
        dma((n_z, 3)),
        dma((n_z, 3)),
        dma((n_z,)),
        dma((n_z,)),
    ] + [pltpu.VMEM(held, BF16)] * (4 * ring)
    vmem = pl.BlockSpec(memory_space=pltpu.VMEM)
    smem = pl.BlockSpec(memory_space=pltpu.SMEM)
    anywhere = pl.BlockSpec(memory_space=pl.ANY)
    return pl.pallas_call(
        functools.partial(kernel, (n_y, n_x, n_z, requests, picked)),
        out_shape=jax.ShapeDtypeStruct(queries.shape, BF16),
        in_specs=[smem, smem, anywhere, anywhere, anywhere, vmem, vmem],
        out_specs=anywhere,
        scratch_shapes=scratch,
        name="retrieve_attend",
        compiler_params=pltpu.CompilerParams(
            collective_id=0, has_side_effects=True, vmem_limit_bytes=56 << 20
        ),
    )(storage_row, retrieved, queries, question_keys, question_values, stored_keys, stored_values)


def solution(mesh):
    return jax.shard_map(
        local,
        mesh=mesh,
        in_specs=(
            P(("store", "mp"), None),
            P(("store", "mp"), None),
            P(("store", "mp"), None),
            P("store", None, "mp"),
            P("store", None, "mp"),
            P(),
            P("store", None),
        ),
        out_specs=P(("store", "mp"), None),
        check_vma=False,
    )
```

time: 603 us -> 108 us (0.18)
  the two profiles are of different devices: /device:TPU:8 before, /device:TPU:1 now
where the time goes in v1:
time: 108 us
  Pallas kernels  106 us (98%)
  local copies, waits for them, and re-layouts  2.26 us (2%)
    pallas_call x1, Pallas kernels, local(): pl.pallas_call(functools.partial(kernel, (n_y, n_x, n_z, requests, picked...  106 us
    unnamed x1, local copies, waits for them, and re-layouts  2.26 us

profile of v1, /device:TPU:1, one launch (start us, length us, event | category | flops | bytes accessed | tf_op | source)
XLA Modules:
  0.0 108.3 jit_solution(1793747891295831348)
XLA Ops:
  0.0 106.0 %retrieve_attend.1 = bf16[64,8192]{1,0:T(8,128)(2,1)} custom-call(s32[512]{0:T(512)} %storage_row.1, s32[4,16]{1,0:T(4,128)} %retrieved.1, bf16[64,8192]{1,0:T(8,128)(2,1)} %queries.1, bf16[64,1024]{1,0:T(8,128)(2,1)} %question_keys.1, bf16[64,1024]{1,0:T(8,128)(2,1)} %question_values.1, bf16[8,128,128]{2,1,0:T(8,128)(2,1)} %stored_keys.1, ...), custom_call_target="tpu_custom_call" | custom-call | tf_op jit(solution)/shard_map/retrieve_attend/pallas_call | solution.py:342
  106.0 2.3 %copy.9 = bf16[64,8192]{1,0:T(8,128)(2,1)} copy(bf16[64,8192]{1,0:T(8,128)(2,1)} %retrieve_attend.1) | data formatting | bytes 2097152

commit v2 on v1

v2 whole, which is shorter than its diff:
```python
import functools
import math

import jax
import jax.numpy as jnp
from jax import lax
from jax.experimental import pallas as pl
from jax.experimental.pallas import tpu as pltpu
from jax.sharding import PartitionSpec as P

HEAD = 128
GROUP = 8
TOKENS = 128
CORES = 2
X_CHIPS = 4
HEADS_AT_ONCE = 2
EXPONENT = math.log2(math.e) / math.sqrt(HEAD)
MESH = pl.DeviceIdType.MESH
BF16 = jnp.bfloat16
F32 = jnp.float32


def score_dot(a, b):
    return lax.dot_general(a, b, (((1,), (1,)), ((), ())), preferred_element_type=F32)


def kernel(
    sizes,
    storage_row,
    retrieved,
    queries,
    question_keys,
    question_values,
    stored_keys,
    stored_values,
    out,
    *scratch,
):
    n_y, n_x, n_z, requests, picked = sizes
    ring = n_y // 2
    members = n_x * CORES
    halves = n_z // requests
    part = TOKENS // halves
    width = GROUP * HEAD
    (
        table,
        tables,
        tables_smem,
        holder_of,
        stage,
        recv,
        q_all,
        kn_all,
        vn_all,
        o_stage,
        scores,
        local_sem,
        table_send,
        table_recv,
        ring_send,
        ring_recv,
        blk_send,
        blk_recv,
        z_send,
        z_recv,
        o_send,
        o_recv,
        keep_sem,
    ) = scratch[:23]
    up_keys, up_values, down_keys, down_values = (
        scratch[23 + ring * i : 23 + ring * (i + 1)] for i in range(4)
    )

    store = lax.axis_index("store")
    z = lax.axis_index("mp")
    y = store // members
    member = store % members
    y_up = lax.rem(y + 1, n_y) * members + member
    y_down = lax.rem(y + n_y - 1, n_y) * members + member

    def peer(j):
        return y * members + lax.rem(member + j, members)

    def z_peer(j):
        return lax.rem(z + j, n_z)

    barrier = pltpu.get_barrier_semaphore()
    for target in (y_up, y_down):
        pl.semaphore_signal(barrier, inc=1, device_id=(target, z), device_id_type=MESH)
    for j in range(1, members):
        pl.semaphore_signal(barrier, inc=1, device_id=(peer(j), z), device_id_type=MESH)
    for j in range(1, n_z):
        pl.semaphore_signal(barrier, inc=1, device_id=(store, z_peer(j)), device_id_type=MESH)

    lane = lax.broadcasted_iota(jnp.int32, (1, 128), 1)

    def note(i, value):
        request, k = i // picked, lax.rem(i, picked)
        row = storage_row[retrieved[request, k]]
        holder_of[request, k] = row // 8
        return jnp.where(lane == row // 8, lax.rem(row, 8), value)

    table[...] = lax.fori_loop(0, requests * picked, note, jnp.zeros((1, 128), jnp.int32))
    pl.semaphore_wait(barrier, 2 + members - 1 + n_z - 1)

    def remote(src, dst, send, recv_sem, device):
        return pltpu.make_async_remote_copy(
            src_ref=src,
            dst_ref=dst,
            send_sem=send,
            recv_sem=recv_sem,
            device_id=device,
            device_id_type=MESH,
        )

    def table_copy(j):
        return remote(
            table, tables.at[member], table_send.at[j], table_recv.at[j], (peer(j), z)
        )

    for j in range(1, members):
        table_copy(j).start()

    def ring_copy(step, way, kind):
        bufs = ((up_keys, up_values), (down_keys, down_values))[way][kind]
        src = (stored_keys, stored_values)[kind] if step == 1 else bufs[step - 2]
        return remote(
            src,
            bufs[step - 1],
            ring_send.at[step - 1, way, kind],
            ring_recv.at[step - 1, way, kind],
            ((y_up, y_down)[way], z),
        )

    def in_ring(step, way, kind):
        return step < ring or (step == ring and way == kind)

    for kind in range(2):
        for way in range(2):
            if in_ring(1, way, kind):
                ring_copy(1, way, kind).start()

    def z_copies(j):
        to = z_peer(j)
        wide = pl.ds(pl.multiple_of(to * width, width), width)
        narrow = pl.ds(pl.multiple_of(to * HEAD, HEAD), HEAD)
        return [
            remote(src, dst, z_send.at[j, n], z_recv.at[j, n], (store, to))
            for n, (src, dst) in enumerate(
                (
                    (queries.at[:, wide], q_all.at[z]),
                    (question_keys.at[:, narrow], kn_all.at[z]),
                    (question_values.at[:, narrow], vn_all.at[z]),
                )
            )
        ]

    tables[member] = table[...]
    for j in range(1, members):
        table_copy(j).wait()
    to_smem = pltpu.make_async_copy(tables, tables_smem, local_sem.at[3])
    to_smem.start()
    to_smem.wait()

    chip, core = member // CORES, lax.rem(member, CORES)
    targets = [
        lax.rem(chip + i, n_x) * CORES + (lax.rem(core + c, CORES) if i == 0 else c)
        for i in range(n_x)
        for c in range(CORES)
    ][1:]

    def hand_out(slot, kind, offset, blocks):
        holder = lax.rem(y + n_y + offset, n_y) * members + member
        for target in targets:
            stage[slot, kind, target] = blocks[tables_smem[target, 0, holder]]
            remote(
                stage.at[slot, kind, target],
                recv.at[holder, kind],
                blk_send.at[target],
                blk_recv.at[member],
                (y * members + target, z),
            ).start()
        recv[holder, kind] = blocks[tables_smem[member, 0, holder]]

    def arrived(parcels):
        for parcel in parcels:
            hand_out(*parcel)

    def all_blocks(other):
        return remote(
            stage.at[:, :, other],
            recv.at[pl.ds(0, n_y)],
            blk_send.at[other],
            blk_recv.at[other],
            (y * members + other, z),
        )

    arrived([(0, 0, 0, stored_keys), (0, 1, 0, stored_values)])
    for j in range(1, n_z):
        for copy in z_copies(j):
            copy.start()
    wide = pl.ds(pl.multiple_of(z * width, width), width)
    narrow = pl.ds(pl.multiple_of(z * HEAD, HEAD), HEAD)
    own = [
        pltpu.make_async_copy(queries.at[:, wide], q_all.at[z], local_sem.at[0]),
        pltpu.make_async_copy(question_keys.at[:, narrow], kn_all.at[z], local_sem.at[1]),
        pltpu.make_async_copy(question_values.at[:, narrow], vn_all.at[z], local_sem.at[2]),
    ]
    for copy in own:
        copy.start()

    for step in range(1, ring + 1):
        for kind in range(2):
            parcels = []
            for way in range(2):
                if in_ring(step, way, kind):
                    ring_copy(step, way, kind).wait_recv()
                    if in_ring(step + 1, way, kind):
                        ring_copy(step + 1, way, kind).start()
                    blocks = ((up_keys, up_values), (down_keys, down_values))[way][kind]
                    slot = 2 * step - 1 + (way if step < ring else 0)
                    parcels.append((slot, kind, (-step, step)[way], blocks[step - 1]))
            arrived(parcels)
    for j in range(1, n_z):
        for copy in z_copies(j):
            copy.wait_recv()
    for copy in own:
        copy.wait()

    for other in targets:
        all_blocks(other).wait_recv()

    rows = HEADS_AT_ONCE * TOKENS
    columns = HEADS_AT_ONCE * HEAD
    far = picked * HEAD
    base = z // halves
    here = lax.rem(z, halves)

    def out_copy(c, source, target):
        mine = pl.ds(pl.multiple_of(z * width + c * columns, columns), columns)
        return remote(
            o_stage.at[target, :, pl.ds(pl.multiple_of(c * columns, columns), columns)],
            out.at[:, mine],
            o_send.at[c, target],
            o_recv.at[c, source],
            (store, target),
        )

    def keep_copy(c):
        mine = pl.ds(pl.multiple_of(z * width + c * columns, columns), columns)
        return pltpu.make_async_copy(
            o_stage.at[z, :, pl.ds(pl.multiple_of(c * columns, columns), columns)],
            out.at[:, mine],
            keep_sem.at[c],
        )

    def heads(c):
        return [
            pl.ds(pl.multiple_of(c * columns + i * HEAD, HEAD), HEAD)
            for i in range(HEADS_AT_ONCE)
        ]

    def score(c, request, buf):
        mine = pl.ds(request * halves, halves)
        q = jnp.concatenate(
            [q_all[mine, :, cols].reshape(TOKENS, HEAD) for cols in heads(c)], axis=0
        )
        near = score_dot(q, kn_all[mine].reshape(TOKENS, HEAD))
        token = lax.rem(lax.broadcasted_iota(jnp.int32, (rows, TOKENS), 0), TOKENS)
        key = lax.broadcasted_iota(jnp.int32, (rows, TOKENS), 1)
        near = jnp.where(key <= token, near, -jnp.inf)
        scores[buf, :, far : far + HEAD] = near
        top = near
        for k in range(0, picked, 2):
            pair = [recv[holder_of[request, k + i], 0] for i in range(2)]
            s = score_dot(q, jnp.concatenate(pair, axis=0))
            scores[buf, :, k * HEAD : (k + 2) * HEAD] = s
            top = jnp.maximum(top, jnp.maximum(s[:, :HEAD], s[:, HEAD:]))
        return jnp.max(top, axis=1, keepdims=True)

    def weigh(c, request, buf, top):
        mine = pl.ds(request * halves, halves)
        w = jnp.exp2((scores[buf, :, far : far + HEAD] - top) * EXPONENT)
        total = w
        summed = jnp.dot(
            w.astype(BF16), vn_all[mine].reshape(TOKENS, HEAD), preferred_element_type=F32
        )
        for k in range(0, picked, 2):
            pair = [recv[holder_of[request, k + i], 1] for i in range(2)]
            w = jnp.exp2((scores[buf, :, k * HEAD : (k + 2) * HEAD] - top) * EXPONENT)
            total = total + (w[:, :HEAD] + w[:, HEAD:])
            summed = summed + jnp.dot(
                w.astype(BF16), jnp.concatenate(pair, axis=0), preferred_element_type=F32
            )
        result = (summed * (1.0 / jnp.sum(total, axis=1, keepdims=True))).astype(BF16)
        for i, cols in enumerate(heads(c)):
            o_stage[mine, :, cols] = result[i * TOKENS : (i + 1) * TOKENS].reshape(
                halves, part, HEAD
            )

    def chunk(c, carry):
        order = [lax.rem(base + i, requests) for i in range(1, requests + 1)]
        top = score(c, order[0], 0)
        for i, request in enumerate(order):
            ahead = score(c, order[i + 1], (i + 1) % 2) if i + 1 < requests else None
            weigh(c, request, i % 2, top)
            top = ahead
            if i + 1 < requests:
                for half in range(halves):
                    out_copy(c, z, request * halves + half).start()
            else:
                keep_copy(c).start()
                for j in range(1, halves):
                    out_copy(c, z, base * halves + lax.rem(here + j, halves)).start()
        return carry

    chunks = GROUP // HEADS_AT_ONCE
    lax.fori_loop(0, chunks, chunk, 0)

    for step in range(1, ring + 1):
        for kind in range(2):
            for way in range(2):
                if in_ring(step, way, kind):
                    ring_copy(step, way, kind).wait_send()
    for j in range(1, n_z):
        for copy in z_copies(j):
            copy.wait_send()
    for other in targets:
        all_blocks(other).wait_send()

    def finish(c, carry):
        keep_copy(c).wait()
        for j in range(1, n_z):
            out_copy(c, z, z_peer(j)).wait_send()
            out_copy(c, z_peer(j), z_peer(j)).wait_recv()
        return carry

    lax.fori_loop(0, chunks, finish, 0)


def local(queries, question_keys, question_values, stored_keys, stored_values, storage_row, retrieved):
    n_store, n_z = lax.axis_size("store"), lax.axis_size("mp")
    n_x = X_CHIPS
    members = n_x * CORES
    n_y = n_store // members
    requests, picked = retrieved.shape
    ring = n_y // 2
    part = queries.shape[0]
    width = GROUP * HEAD
    held = stored_keys.shape
    chunks = GROUP // HEADS_AT_ONCE
    dma = pltpu.SemaphoreType.DMA
    scratch = [
        pltpu.VMEM((1, 128), jnp.int32),
        pltpu.VMEM((members, 1, 128), jnp.int32),
        pltpu.SMEM((members, 1, 128), jnp.int32),
        pltpu.SMEM((requests, picked), jnp.int32),
        pltpu.VMEM((n_y, 2, members, TOKENS, HEAD), BF16),
        pltpu.VMEM((n_store, 2, TOKENS, HEAD), BF16),
        pltpu.VMEM((n_z, part, width), BF16),
        pltpu.VMEM((n_z, part, HEAD), BF16),
        pltpu.VMEM((n_z, part, HEAD), BF16),
        pltpu.VMEM((n_z, part, width), BF16),
        pltpu.VMEM((2, HEADS_AT_ONCE * TOKENS, (picked + 1) * HEAD), F32),
        dma((5,)),
        dma((members,)),
        dma((members,)),
        dma((ring, 2, 2)),
        dma((ring, 2, 2)),
        dma((members,)),
        dma((members,)),
        dma((n_z, 3)),
        dma((n_z, 3)),
        dma((chunks, n_z)),
        dma((chunks, n_z)),
        dma((chunks,)),
    ] + [pltpu.VMEM(held, BF16)] * (4 * ring)
    vmem = pl.BlockSpec(memory_space=pltpu.VMEM)
    smem = pl.BlockSpec(memory_space=pltpu.SMEM)
    anywhere = pl.BlockSpec(memory_space=pl.ANY)
    return pl.pallas_call(
        functools.partial(kernel, (n_y, n_x, n_z, requests, picked)),
        out_shape=jax.ShapeDtypeStruct(queries.shape, BF16),
        in_specs=[smem, smem, anywhere, anywhere, anywhere, vmem, vmem],
        out_specs=anywhere,
        scratch_shapes=scratch,
        name="retrieve_attend",
        compiler_params=pltpu.CompilerParams(
            collective_id=0, has_side_effects=True, vmem_limit_bytes=56 << 20
        ),
    )(storage_row, retrieved, queries, question_keys, question_values, stored_keys, stored_values)


def solution(mesh):
    return jax.shard_map(
        local,
        mesh=mesh,
        in_specs=(
            P(("store", "mp"), None),
            P(("store", "mp"), None),
            P(("store", "mp"), None),
            P("store", None, "mp"),
            P("store", None, "mp"),
            P(),
            P("store", None),
        ),
        out_specs=P(("store", "mp"), None),
        check_vma=False,
    )
```

time: 108 us -> 95.3 us (0.88)
  Pallas kernels: 106 us -> 92.8 us
    pallas_call x1, Pallas kernels: 106 us -> 92.8 us  [local(): pl.pallas_call(functools.partial(kernel, (n_y, n_x, n_z, requests, picked...]
where the time goes in v2:
time: 95.3 us; the launch traced here: 95 us
  Pallas kernels  92.8 us (97%)
  local copies, waits for them, and re-layouts  2.26 us (2%)
    pallas_call x1, Pallas kernels, local(): pl.pallas_call(functools.partial(kernel, (n_y, n_x, n_z, requests, picked...  92.8 us
    unnamed x1, local copies, waits for them, and re-layouts  2.26 us

profile of v2, /device:TPU:1, one launch (start us, length us, event | category | flops | bytes accessed | tf_op | source)
XLA Modules:
  0.0 95.0 jit_solution(13378070454799795817)
XLA Ops:
  0.0 92.8 %retrieve_attend.1 = bf16[64,8192]{1,0:T(8,128)(2,1)} custom-call(s32[512]{0:T(512)} %storage_row.1, s32[4,16]{1,0:T(4,128)} %retrieved.1, bf16[64,8192]{1,0:T(8,128)(2,1)} %queries.1, bf16[64,1024]{1,0:T(8,128)(2,1)} %question_keys.1, bf16[64,1024]{1,0:T(8,128)(2,1)} %question_values.1, bf16[8,128,128]{2,1,0:T(8,128)(2,1)} %stored_keys.1, ...), custom_call_target="tpu_custom_call" | custom-call | tf_op jit(solution)/shard_map/retrieve_attend/pallas_call | solution.py:381
  92.8 2.3 %copy.9 = bf16[64,8192]{1,0:T(8,128)(2,1)} copy(bf16[64,8192]{1,0:T(8,128)(2,1)} %retrieve_attend.1) | data formatting | bytes 2097152

commit v3 on v2

--- a/solution.py
+++ b/solution.py
@@ -380,9 +380,9 @@
     anywhere = pl.BlockSpec(memory_space=pl.ANY)
     return pl.pallas_call(
         functools.partial(kernel, (n_y, n_x, n_z, requests, picked)),
-        out_shape=jax.ShapeDtypeStruct(queries.shape, BF16),
+        out_shape=pltpu.VMEM(queries.shape, BF16),
         in_specs=[smem, smem, anywhere, anywhere, anywhere, vmem, vmem],
-        out_specs=anywhere,
+        out_specs=vmem,
         scratch_shapes=scratch,
         name="retrieve_attend",
         compiler_params=pltpu.CompilerParams(

time: 95.3 us -> 93.8 us (0.984)
  local copies, waits for them, and re-layouts: 2.26 us -> 0.97 us
    unnamed x1, local copies, waits for them, and re-layouts: 2.26 us -> 0.97 us
where the time goes in v3:
time: 93.8 us; the launch traced here: 93.7 us
  Pallas kernels  92.7 us (99%)
  local copies, waits for them, and re-layouts  0.97 us (1%)
    pallas_call x1, Pallas kernels, local(): pl.pallas_call(functools.partial(kernel, (n_y, n_x, n_z, requests, picked...  92.7 us

profile of v3, /device:TPU:1, one launch (start us, length us, event | category | flops | bytes accessed | tf_op | source)
XLA Modules:
  0.0 93.7 jit_solution(11808886028702587201)
XLA Ops:
  0.0 92.7 %retrieve_attend.1 = bf16[64,8192]{1,0:T(8,128)(2,1)S(1)} custom-call(s32[512]{0:T(512)} %storage_row.1, s32[4,16]{1,0:T(4,128)} %retrieved.1, bf16[64,8192]{1,0:T(8,128)(2,1)} %queries.1, bf16[64,1024]{1,0:T(8,128)(2,1)} %question_keys.1, bf16[64,1024]{1,0:T(8,128)(2,1)} %question_values.1, bf16[8,128,128]{2,1,0:T(8,128)(2,1)} %stored_keys.1, ...), custom_call_target="tpu_custom_call" | custom-call | tf_op jit(solution)/shard_map/retrieve_attend/pallas_call | solution.py:381
  92.7 1.0 %copy.9 = bf16[64,8192]{1,0:T(8,128)(2,1)} copy(bf16[64,8192]{1,0:T(8,128)(2,1)S(1)} %retrieve_attend.1) | data formatting | bytes 2097152

commit v4 on v3

--- a/solution.py
+++ b/solution.py
@@ -48,7 +48,8 @@
         tables_smem,
         holder_of,
         stage,
-        recv,
+        far_keys,
+        far_values,
         q_all,
         kn_all,
         vn_all,
@@ -66,9 +67,9 @@
         o_send,
         o_recv,
         keep_sem,
-    ) = scratch[:23]
+    ) = scratch[:24]
     up_keys, up_values, down_keys, down_values = (
-        scratch[23 + ring * i : 23 + ring * (i + 1)] for i in range(4)
+        scratch[24 + ring * i : 24 + ring * (i + 1)] for i in range(4)
     )
 
     store = lax.axis_index("store")
@@ -169,29 +170,31 @@
         for c in range(CORES)
     ][1:]
 
+    far = (far_keys, far_values)
+
     def hand_out(slot, kind, offset, blocks):
         holder = lax.rem(y + n_y + offset, n_y) * members + member
         for target in targets:
             stage[slot, kind, target] = blocks[tables_smem[target, 0, holder]]
             remote(
                 stage.at[slot, kind, target],
-                recv.at[holder, kind],
-                blk_send.at[target],
-                blk_recv.at[member],
+                far[kind].at[holder],
+                blk_send.at[kind, target],
+                blk_recv.at[kind, member],
                 (y * members + target, z),
             ).start()
-        recv[holder, kind] = blocks[tables_smem[member, 0, holder]]
+        far[kind][holder] = blocks[tables_smem[member, 0, holder]]
 
     def arrived(parcels):
         for parcel in parcels:
             hand_out(*parcel)
 
-    def all_blocks(other):
+    def all_blocks(kind, other):
         return remote(
-            stage.at[:, :, other],
-            recv.at[pl.ds(0, n_y)],
-            blk_send.at[other],
-            blk_recv.at[other],
+            stage.at[:, kind, other],
+            far[kind].at[pl.ds(0, n_y)],
+            blk_send.at[kind, other],
+            blk_recv.at[kind, other],
             (y * members + other, z),
         )
 
@@ -228,11 +231,11 @@
         copy.wait()
 
     for other in targets:
-        all_blocks(other).wait_recv()
+        all_blocks(0, other).wait_recv()
 
     rows = HEADS_AT_ONCE * TOKENS
     columns = HEADS_AT_ONCE * HEAD
-    far = picked * HEAD
+    near_at = picked * HEAD
     base = z // halves
     here = lax.rem(z, halves)
 
@@ -269,10 +272,10 @@
         token = lax.rem(lax.broadcasted_iota(jnp.int32, (rows, TOKENS), 0), TOKENS)
         key = lax.broadcasted_iota(jnp.int32, (rows, TOKENS), 1)
         near = jnp.where(key <= token, near, -jnp.inf)
-        scores[buf, :, far : far + HEAD] = near
+        scores[buf, :, near_at : near_at + HEAD] = near
         top = near
         for k in range(0, picked, 2):
-            pair = [recv[holder_of[request, k + i], 0] for i in range(2)]
+            pair = [far_keys[holder_of[request, k + i]] for i in range(2)]
             s = score_dot(q, jnp.concatenate(pair, axis=0))
             scores[buf, :, k * HEAD : (k + 2) * HEAD] = s
             top = jnp.maximum(top, jnp.maximum(s[:, :HEAD], s[:, HEAD:]))
@@ -280,13 +283,13 @@
 
     def weigh(c, request, buf, top):
         mine = pl.ds(request * halves, halves)
-        w = jnp.exp2((scores[buf, :, far : far + HEAD] - top) * EXPONENT)
+        w = jnp.exp2((scores[buf, :, near_at : near_at + HEAD] - top) * EXPONENT)
         total = w
         summed = jnp.dot(
             w.astype(BF16), vn_all[mine].reshape(TOKENS, HEAD), preferred_element_type=F32
         )
         for k in range(0, picked, 2):
-            pair = [recv[holder_of[request, k + i], 1] for i in range(2)]
+            pair = [far_values[holder_of[request, k + i]] for i in range(2)]
             w = jnp.exp2((scores[buf, :, k * HEAD : (k + 2) * HEAD] - top) * EXPONENT)
             total = total + (w[:, :HEAD] + w[:, HEAD:])
             summed = summed + jnp.dot(
@@ -298,11 +301,13 @@
                 halves, part, HEAD
             )
 
-    def chunk(c, carry):
+    def chunk(c, top):
         order = [lax.rem(base + i, requests) for i in range(1, requests + 1)]
-        top = score(c, order[0], 0)
         for i, request in enumerate(order):
-            ahead = score(c, order[i + 1], (i + 1) % 2) if i + 1 < requests else None
+            if i + 1 < requests:
+                ahead = score(c, order[i + 1], (i + 1) % 2)
+            else:
+                ahead = score(jnp.minimum(c + 1, chunks - 1), order[0], 0)
             weigh(c, request, i % 2, top)
             top = ahead
             if i + 1 < requests:
@@ -312,10 +317,13 @@
                 keep_copy(c).start()
                 for j in range(1, halves):
                     out_copy(c, z, base * halves + lax.rem(here + j, halves)).start()
-        return carry
+        return top
 
     chunks = GROUP // HEADS_AT_ONCE
-    lax.fori_loop(0, chunks, chunk, 0)
+    top = score(0, lax.rem(base + 1, requests), 0)
+    for other in targets:
+        all_blocks(1, other).wait_recv()
+    lax.fori_loop(0, chunks, chunk, top)
 
     for step in range(1, ring + 1):
         for kind in range(2):
@@ -325,8 +333,9 @@
     for j in range(1, n_z):
         for copy in z_copies(j):
             copy.wait_send()
-    for other in targets:
-        all_blocks(other).wait_send()
+    for kind in range(2):
+        for other in targets:
+            all_blocks(kind, other).wait_send()
 
     def finish(c, carry):
         keep_copy(c).wait()
@@ -356,7 +365,8 @@
         pltpu.SMEM((members, 1, 128), jnp.int32),
         pltpu.SMEM((requests, picked), jnp.int32),
         pltpu.VMEM((n_y, 2, members, TOKENS, HEAD), BF16),
-        pltpu.VMEM((n_store, 2, TOKENS, HEAD), BF16),
+        pltpu.VMEM((n_store, TOKENS, HEAD), BF16),
+        pltpu.VMEM((n_store, TOKENS, HEAD), BF16),
         pltpu.VMEM((n_z, part, width), BF16),
         pltpu.VMEM((n_z, part, HEAD), BF16),
         pltpu.VMEM((n_z, part, HEAD), BF16),
@@ -367,8 +377,8 @@
         dma((members,)),
         dma((ring, 2, 2)),
         dma((ring, 2, 2)),
-        dma((members,)),
-        dma((members,)),
+        dma((2, members)),
+        dma((2, members)),
         dma((n_z, 3)),
         dma((n_z, 3)),
         dma((chunks, n_z)),

time: 93.8 us -> 93.5 us (level)
  no operation moved by 1% of the time
where the time goes in v4:
time: 93.5 us; the launch traced here: 93.4 us
  Pallas kernels  92.4 us (99%)
  local copies, waits for them, and re-layouts  0.97 us (1%)
    pallas_call x1, Pallas kernels, local(): pl.pallas_call(functools.partial(kernel, (n_y, n_x, n_z, requests, picked...  92.4 us

profile of v4, /device:TPU:1, one launch (start us, length us, event | category | flops | bytes accessed | tf_op | source)
XLA Modules:
  0.0 93.4 jit_solution(2392465488917305312)
XLA Ops:
  0.0 92.4 %retrieve_attend.1 = bf16[64,8192]{1,0:T(8,128)(2,1)S(1)} custom-call(s32[512]{0:T(512)} %storage_row.1, s32[4,16]{1,0:T(4,128)} %retrieved.1, bf16[64,8192]{1,0:T(8,128)(2,1)} %queries.1, bf16[64,1024]{1,0:T(8,128)(2,1)} %question_keys.1, bf16[64,1024]{1,0:T(8,128)(2,1)} %question_values.1, bf16[8,128,128]{2,1,0:T(8,128)(2,1)} %stored_keys.1, ...), custom_call_target="tpu_custom_call" | custom-call | tf_op jit(solution)/shard_map/retrieve_attend/pallas_call | solution.py:391
  92.4 1.0 %copy.9 = bf16[64,8192]{1,0:T(8,128)(2,1)} copy(bf16[64,8192]{1,0:T(8,128)(2,1)S(1)} %retrieve_attend.1) | data formatting | bytes 2097152
